TPU v7x, 32 devices: a whole 2x2x4 slice. The times are simulated.
32 devices in a mesh: gz: 4 (over y, core), xy: 8 (over z, x).
Axes of the slice: x: 2, y: 2, z: 4, core: 2. Of those that a mesh axis runs over, the one named last changes fastest.
Arguments:
- cotangent: bfloat16 [4, 8, 9, 128, 128], P('gz', 'xy'), may hold values from -6 to 6
- displacement: float32 [4, 8, 3, 32, 128], P('gz', 'xy'), may hold values from -2 to 2
- neighbours: int32 [4, 8, 32, 128], P('gz', 'xy'), may hold values from 0 to 2303
- counts: int32 [4, 8, 128], P('gz', 'xy'), may hold values from 8 to 32, as said below
- atom_feat: bfloat16 [4, 8, 256, 128], P('gz', 'xy'), may hold values from -6 to 6
- radial_weight: float32 [3, 16, 128], replicated, may hold values from -1.5 to 1.5
- mix_weight: bfloat16 [3, 128, 128], replicated, may hold values from -0.5 to 0.5
Outputs:
- atom_grad: float32 [4, 8, 256, 128], P('gz', 'xy')
- radial_grad: float32 [3, 16, 128], replicated
- mix_grad: float32 [3, 128, 128], replicated
Inputs may be any that keep to these rules, and one draw needn't show every extreme that they name: `counts`: the first probe of the first brick uses all 32 slots and the first probe of the second brick uses 32 // 4.
All inputs are finite; a program needn't handle non-finite values.
Results may differ from a plain program's by a relative error of at most 0.0051.
Values may be sent and summed in bfloat16 or wider, within the bound.
A program may use at most 64 MiB of HBM per device.

v0:
```python
import math
import jax
import jax.numpy as jnp
from jax import lax
from jax.sharding import PartitionSpec as P

CUTOFF = 4.0
LEVEL_SPANS = ((0, 1), (1, 4), (4, 9))


def padded(cells, sides, width):
    for axis, dim in sides:
        count = lax.axis_size(axis)
        head = lax.slice_in_dim(cells, 0, width, axis=dim)
        tail = lax.slice_in_dim(cells, cells.shape[dim] - width, cells.shape[dim], axis=dim)
        cells = jnp.concatenate(
            [
                lax.ppermute(tail, axis, [(i, (i + 1) % count) for i in range(count)]),
                cells,
                lax.ppermute(head, axis, [((i + 1) % count, i) for i in range(count)]),
            ],
            axis=dim,
        )
    return cells


def harmonics(disp):
    scaled = disp / CUTOFF
    coord_x, coord_y, coord_z = (scaled[0], scaled[1], scaled[2])
    root3, root5, root15 = (math.sqrt(3.0), math.sqrt(5.0), math.sqrt(15.0))
    return jnp.stack(
        [
            jnp.ones_like(coord_x),
            root3 * coord_x,
            root3 * coord_y,
            root3 * coord_z,
            root15 * coord_x * coord_y,
            root15 * coord_y * coord_z,
            0.5 * root5 * (2.0 * coord_z * coord_z - coord_x * coord_x - coord_y * coord_y),
            root15 * coord_x * coord_z,
            0.5 * root15 * (coord_x * coord_x - coord_y * coord_y),
        ]
    )


def basis(disp, nbasis):
    distance = jnp.sqrt(jnp.sum(disp * disp, axis=0))
    centres = jnp.arange(nbasis).astype(jnp.float32) * (CUTOFF / (nbasis - 1))
    sharpness = ((nbasis - 1) / CUTOFF) ** 2
    envelope = 0.5 * (jnp.cos(math.pi * distance / CUTOFF) + 1.0)
    shaped = centres.reshape((nbasis,) + (1,) * distance.ndim)
    return jnp.exp(-sharpness * (distance[None] - shaped) ** 2) * envelope[None]


def exact(form, left, right):
    return jnp.einsum(form, left, right, precision=lax.Precision.HIGHEST)


def matmul(form, left, right):
    return jnp.einsum(form, left, right, preferred_element_type=jnp.float32)


def gate_backward(moments, mix_weight, cotangent):
    mixed_out = [
        matmul("mpc,cd->mpd", moments[span_start:span_end], mix_weight[level])
        for level, (span_start, span_end) in enumerate(LEVEL_SPANS)
    ]
    scalar = mixed_out[0][0]
    gating = jax.nn.sigmoid(scalar)
    gate_slope = gating * (1.0 - gating)
    cot_float = cotangent.astype(jnp.float32)
    higher = jnp.concatenate(mixed_out[1:], 0)
    first_term = (
        cot_float[0] * (gating + scalar * gate_slope)
        + jnp.sum(cot_float[1:] * higher, 0) * gate_slope
    )
    dmixed = jnp.concatenate([first_term[None], cot_float[1:] * gating[None]], 0).astype(
        jnp.bfloat16
    )
    dmoments = jnp.concatenate(
        [
            matmul("mpd,cd->mpc", dmixed[span_start:span_end], mix_weight[level])
            for level, (span_start, span_end) in enumerate(LEVEL_SPANS)
        ],
        0,
    ).astype(jnp.bfloat16)
    mix_part = jnp.stack(
        [
            matmul("mpc,mpd->cd", moments[span_start:span_end], dmixed[span_start:span_end])
            for span_start, span_end in LEVEL_SPANS
        ]
    )
    return (dmoments, mix_part)


def shards(cotangent, displacement, neighbours, counts, atom_feat, radial_weight, mix_weight):
    cot_local = cotangent[0, 0]
    disp_local = displacement[0, 0]
    neighbour_local_index = neighbours[0, 0]
    probe_tally = counts[0, 0]
    slot_count = neighbour_local_index.shape[0]
    probe_count = neighbour_local_index.shape[1]
    natom = atom_feat.shape[2]
    channels = atom_feat.shape[3]
    nbasis = radial_weight.shape[1]
    filled_slots = (
        lax.broadcasted_iota(jnp.int32, (slot_count, probe_count), 0) < probe_tally[None]
    ).astype(jnp.float32)
    angular = harmonics(disp_local) * filled_slots[None]
    radial_basis = basis(disp_local, nbasis)
    atom_table = padded(atom_feat, (("gz", 0), ("xy", 1)), 1).reshape(9 * natom, channels)
    features = atom_table[neighbour_local_index].astype(jnp.float32)
    radial = exact("bkp,lbc->lkpc", radial_basis, radial_weight)
    pieces = []
    for level, (span_start, span_end) in enumerate(LEVEL_SPANS):
        weighted = radial[level] * features
        pieces.append(jnp.sum(angular[span_start:span_end, :, :, None] * weighted[None], axis=1))
    moments = jnp.concatenate(pieces, 0).astype(jnp.bfloat16)
    dmoments, mix_part = gate_backward(moments, mix_weight, cot_local)
    mix_total = lax.psum(mix_part, ("gz", "xy"))
    dmoment_float = dmoments.astype(jnp.float32)
    contrib = jnp.zeros(features.shape, jnp.float32)
    radial_parts = []
    for level, (span_start, span_end) in enumerate(LEVEL_SPANS):
        traced = jnp.sum(
            angular[span_start:span_end, :, :, None] * dmoment_float[span_start:span_end, None],
            axis=0,
        )
        contrib = contrib + radial[level] * traced
        radial_parts.append(exact("bkp,kpc->bc", radial_basis, features * traced))
    grads = (
        jnp.zeros((9 * natom, channels), jnp.float32)
        .at[neighbour_local_index.reshape(-1)]
        .add(contrib.reshape(-1, channels))
    )
    radial_part = jnp.stack(radial_parts)
    radial_total = lax.psum(radial_part, ("gz", "xy"))
    blocks = grads.reshape(3, 3, natom, channels)
    outer_rows = jnp.stack([blocks[0], blocks[2]], 0)
    arrived = padded(outer_rows, (("gz", 0),), 1)
    columns = blocks[1] + arrived[0] + arrived[3]
    outer_columns = jnp.stack([columns[0], columns[2]], 0)
    landed = padded(outer_columns, (("xy", 0),), 1)
    owned = columns[1] + landed[0] + landed[3]
    return (owned[None, None], radial_total, mix_total)


def solution(mesh):
    in_specs = (
        P("gz", "xy", None, None, None),
        P("gz", "xy", None, None, None),
        P("gz", "xy", None, None),
        P("gz", "xy", None),
        P("gz", "xy", None, None),
        P(),
        P(),
    )
    out_specs = (P("gz", "xy", None, None), P(), P())
    return jax.shard_map(shards, mesh=mesh, in_specs=in_specs, out_specs=out_specs, check_vma=False)
```

profile of v0, /device:TPU:10, one launch (start us, length us, event | category | flops | bytes accessed | tf_op | source)
XLA Modules:
  0.0 237.2 jit_solution(9430039311791269466)
XLA Ops:
  7.2 0.0 copy-start
  7.2 0.0 all-reduce.2.cloned.1.call-start
  7.2 0.1 collective-permute-start
  7.3 1.7 collective-permute-start.1
  9.0 0.8 multiply_reduce_fusion.5
  9.9 0.7 fusion.78
  10.6 0.1 fusion.86
  10.7 1.3 compare_select_fusion
  12.1 0.0 copy-start.4
  12.1 0.0 copy-start.6
  12.1 0.0 copy-start.7
  12.1 7.2 %convolution_bitcast_fusion = f32[3,32,128,128]{3,2,0,1:T(8,128)} fusion(f32[32,128]{1,0:T(8,128)S(1)} %get-tuple-element.23, f32[16]{0:T(128)S(1)} %convert_multiply_fusion, f32[32,128]{1,0:T(8,128)S(1)} %get-tuple-element.22, f32[3,16,128]{2,1,0:T(8,128)S(1)} %copy-done), kind=kOutput, calls=%fused_computation.6 | convolution fusion | flops 302252032 | bytes 6348864 | tf_op jit(solution)/shard_map/bkp,lbc->lkpc/dot_general | solution.py:56
  19.4 0.9 convert_element_type.43
  20.2 0.0 collective-permute-done
  20.3 0.0 collective-permute-done.1
  20.3 1.6 collective-permute-start.2
  21.9 0.5 collective-permute-start.3
  22.4 8.9 %collective-permute-done.2 = bf16[3,1,256,128]{3,2,1,0:T(8,128)(2,1)S(1)} collective-permute-done((bf16[3,1,256,128]{3,2,1,0:T(8,128)(2,1)S(1)}, bf16[3,1,256,128]{3,2,1,0:T(8,128)(2,1)S(1)}, u32[]{:S(2)}, u32[]{:S(2)}) %collective-permute-start.2) | collective-permute-done | bytes 196640 | tf_op jit(solution)/shard_map/ppermute | solution.py:18
  31.3 0.0 collective-permute-done.3
  31.3 0.1 pad_maximum_fusion
  31.4 12.1 %gather_fusion = bf16[4096,128]{1,0:T(8,128)(2,1)S(1)} fusion(bf16[2304,128]{1,0:T(8,128)(2,1)S(1)} %bitcast.167, s32[4096]{0:T(1024)S(1)} %fusion.74), kind=kCustom, calls=%fused_computation | custom fusion | bytes 2113536 | tf_op jit(solution)/shard_map/gather | solution.py:112
  43.5 0.1 convert_element_type.49
  43.7 3.6 %fusion.83 = (f32[1,32,128,128]{3,2,0,1:T(8,128)S(1)}, bf16[128,128]{1,0:T(8,128)(2,1)S(1)}, f32[32,128,128]{2,1,0:T(8,128)S(1)}, f32[32,128,128]{2,1,0:T(8,128)...) fusion(f32[3,32,128,128]{3,2,0,1:T(8,128)} %convolution_bitcast_fusion, ...), kind=kLoop, calls=%fused_computation.141 | loop fusion | flops 3129344 | bytes 19972096 | tf_op jit(solution)/shard_map/slice | solution.py:129
  47.3 0.0 copy-start.5
  47.3 2.0 multiply_reduce_fusion.3
  49.3 0.1 fusion.54
  49.4 3.1 %multiply_reduce_fusion.1 = bf16[5,128,128]{2,1,0:T(8,128)(2,1)S(1)} fusion(f32[32,128,128]{2,1,0:T(8,128)S(1)} %get-tuple-element.7, f32[5,32,128]{2,1,0:T(8,128)S(1)} %slice.162), kind=kLoop, calls=%fused_computation.3 | loop fusion | flops 5160960 | bytes 2342912 | tf_op jit(solution)/shard_map/reduce_sum | solution.py:117
  52.6 0.2 fusion.48
  52.7 0.2 add_divide_fusion
  52.9 0.1 fusion.24
  53.0 0.2 convolution_bitcast_fusion.2
  53.2 0.2 convolution_bitcast_fusion.1
  53.5 0.2 convolution_convert_fusion
  53.7 0.2 convolution_convert_fusion.1
  53.9 0.0 copy-start.9
  53.9 0.1 fusion.52
  53.9 0.1 fusion.10
  54.1 2.1 multiply_reduce_fusion.2
  56.3 2.1 fusion.11
  58.4 2.0 fusion.14
  60.4 3.2 %multiply_reduce_fusion = f32[32,128,128]{2,1,0:T(8,128)S(1)} fusion(f32[5,128,128]{2,1,0:T(8,128)S(1)} %fusion.27, f32[5,32,128]{2,1,0:T(8,128)S(1)} %slice.162), kind=kLoop, calls=%fused_computation.2 | loop fusion | flops 4718592 | bytes 2506752 | tf_op jit(solution)/shard_map/reduce_sum | solution.py:125
  63.6 2.4 %fusion = f32[4096,128]{1,0:T(8,128)} fusion(f32[32,128,128]{2,1,0:T(8,128)S(1)} %multiply_reduce_fusion, f32[1,32,128,128]{3,2,0,1:T(8,128)S(1)} %get-tuple-element.9, f32[32,128,128]{2,1,0:T(8,128)S(1)} %multiply_reduce_fusion.2, f32[1,32,128,128]{3,2,0,1:T(8,128)S(1)} %get-tuple-element.10, f32[1,32,128,128]{3,2,0,1:T(8,128)S(1)} %get-tuple-element.5, ...), kind=kLoop, calls=%fused_computation.8 | loop fusion | flops 3145728 | bytes 12664832 | tf_op jit(solution)/shard_map/add | solution.py:129
  66.1 0.0 copy-done.1
  66.1 22.9 %scatter_custom_fusion = f32[2304,128]{1,0:T(8,128)S(1)} fusion(s32[4096]{0:T(1024)} %bitcast.176, f32[4096,128]{1,0:T(8,128)} %fusion, f32[]{:T(128)} %constant.14.clone.1), kind=kCustom, calls=%fused_computation.36 | custom fusion | flops 524288 | bytes 1180160 | tf_op jit(solution)/shard_map/scatter-add | solution.py:134
  89.0 0.1 fusion.84
  89.1 0.1 collective-permute-start.4
  89.2 1.7 collective-permute-start.5
  90.9 0.2 convolution_bitcast_fusion.3
  91.1 0.0 copy-done.12
  91.1 1.3 fusion.17
  92.5 0.0 copy-start.10
  92.5 7.3 %collective-permute-done.4 = f32[1,3,256,128]{3,2,1,0:T(8,128)S(1)} collective-permute-done((f32[1,3,256,128]{3,2,1,0:T(8,128)S(1)}, f32[1,3,256,128]{3,2,1,0:T(8,128)S(1)}, u32[]{:S(2)}, u32[]{:S(2)}) %collective-permute-start.4) | collective-permute-done | bytes 393248 | tf_op jit(solution)/shard_map/ppermute | solution.py:18
  99.8 0.0 collective-permute-done.5
  99.8 0.1 bitcast_add_fusion
  99.9 2.5 %collective-permute-start.6 = (f32[1,256,128]{2,1,0:T(8,128)S(1)}, f32[1,256,128]{2,1,0:T(8,128)S(1)}, u32[]{:S(2)}, u32[]{:S(2)}) collective-permute-start(f32[1,256,128]{2,1,0:T(8,128)S(1)} %get-tuple-element.16), channel_id=1, source_target_pairs={{0,1},{1,2},{2,3},{3,4},{4,5},{5,6},{6,7},{7,0},{8,9},{9,10},{10,1... | collective-permute-start | bytes 393224 | tf_op jit(solution)/shard_map/ppermute | solution.py:18
  102.4 0.0 collective-permute-start.7
  102.4 0.7 pad_maximum_fusion.1
  103.1 0.0 all-reduce.2.cloned.1.call-update
  103.1 43.0 %psum.14 = f32[3,16,128]{2,1,0:T(8,128)} all-reduce(f32[3,16,128]{2,1,0:T(8,128)S(1)} %pad_maximum_fusion.4), channel_id=1, replica_groups=mesh['gz'=4,'xy'=8] {'gz','xy'}, use_global_device_ids=true, to_apply=%region_8.0 | all-reduce | flops 6144 | bytes 49152 | tf_op jit(solution)/shard_map/psum | solution.py:137
  146.1 0.0 collective-permute-done.6
  146.1 0.0 collective-permute-done.7
  146.1 0.7 fusion.29
  146.8 81.9 %all-reduce.2.cloned.1.call-done = f32[3,128,128]{2,1,0:T(8,128)} async-done(((f32[3,128,128]{2,1,0:T(8,128)}), f32[3,128,128]{2,1,0:T(8,128)}) %all-reduce.2.cloned.1.call-update) | async-done | bytes 196624 | tf_op jit(solution)/shard_map/psum | solution.py:120
  228.7 1.6 copy.28
  (40 shorter events, 0.3 us)
Async XLA Ops:
  7.2 4.9 %copy-start = (f32[3,16,128]{2,1,0:T(8,128)S(1)}, f32[3,16,128]{2,1,0:T(8,128)}, u32[]{:S(2)}) copy-start(f32[3,16,128]{2,1,0:T(8,128)} %param.12) | copy-start | bytes 73732
  7.2 221.5 %all-reduce.2.cloned.1.call-start = ((), (), s32[]{:S(2)}) async-start(), calls=%async_computation | async-start | bytes 393216 | tf_op jit(solution)/shard_map/psum | solution.py:120
  7.2 13.0 %collective-permute-start = (bf16[1,1,256,128]{3,2,1,0:T(8,128)(2,1)}, bf16[1,1,256,128]{3,2,1,0:T(8,128)(2,1)S(1)}, u32[]{:S(2)}, u32[]{:S(2)}) collective-permute-start(bf16[1,1,256,128]{3,2,1,0:T(8,128)(2,1)} %param.11), channel_id=1, source_target_pairs={{0,8},{8,16},{16,24},{24,0},{1,9},{9,17},{17,25},{25,1},{2,10},{10... | collective-permute-start | bytes 196616 | tf_op jit(solution)/shard_map/ppermute | solution.py:18
  7.3 13.0 %collective-permute-start.1 = (bf16[1,1,256,128]{3,2,1,0:T(8,128)(2,1)}, bf16[1,1,256,128]{3,2,1,0:T(8,128)(2,1)S(1)}, u32[]{:S(2)}, u32[]{:S(2)}) collective-permute-start(bf16[1,1,256,128]{3,2,1,0:T(8,128)(2,1)} %param.11), channel_id=1, source_target_pairs={{8,0},{16,8},{24,16},{0,24},{9,1},{17,9},{25,17},{1,25},{10,2},{18... | collective-permute-start | bytes 196616 | tf_op jit(solution)/shard_map/ppermute | solution.py:20
  9.0 47.2 %copy-start.11 = (f32[16]{0:T(128)}, f32[16]{0:T(128)S(1)}, u32[]{:S(2)}) copy-start(f32[16]{0:T(128)S(1)} %convert_multiply_fusion) | copy-start | bytes 196
  12.1 7.3 %copy-start.4 = (bf16[1,1,9,128,128]{4,3,2,1,0:T(8,128)(2,1)S(1)}, bf16[1,1,9,128,128]{4,3,2,1,0:T(8,128)(2,1)}, u32[]{:S(2)}) copy-start(bf16[1,1,9,128,128]{4,3,2,1,0:T(8,128)(2,1)} %param.7) | copy-start | bytes 884740
  12.1 8.2 %copy-start.6 = (bf16[1,1,256,128]{3,2,1,0:T(8,128)(2,1)S(1)}, bf16[1,1,256,128]{3,2,1,0:T(8,128)(2,1)}, u32[]{:S(2)}) copy-start(bf16[1,1,256,128]{3,2,1,0:T(8,128)(2,1)} %param.11) | copy-start | bytes 196612
  12.1 10.3 %copy-start.7 = (s32[1,1,32,128]{3,2,1,0:T(8,128)S(1)}, s32[1,1,32,128]{3,2,1,0:T(8,128)}, u32[]{:S(2)}) copy-start(s32[1,1,32,128]{3,2,1,0:T(8,128)} %param.9) | copy-start | bytes 49156
  19.3 24.3 %copy-start.8 = (f32[32,128]{1,0:T(8,128)}, f32[32,128]{1,0:T(8,128)S(1)}, u32[]{:S(2)}) copy-start(f32[32,128]{1,0:T(8,128)S(1)} %get-tuple-element.19) | copy-start | bytes 49156
  20.3 11.0 %collective-permute-start.2 = (bf16[3,1,256,128]{3,2,1,0:T(8,128)(2,1)S(1)}, bf16[3,1,256,128]{3,2,1,0:T(8,128)(2,1)S(1)}, u32[]{:S(2)}, u32[]{:S(2)}) collective-permute-start(bf16[3,1,256,128]{3,2,1,0:T(8,128)(2,1)S(1)} %constant_dynamic-update-slice_fusion.9), channel_id=1, source_target_pairs={{0,1},{1,2},{2,3},{3,4},{4,5},{5,6},{6,7},{7,0},{8,9},{9,10},{10,1... | collective-permute-start | bytes 589832 | tf_op jit(solution)/shard_map/ppermute | solution.py:18
  21.9 9.4 %collective-permute-start.3 = (bf16[3,1,256,128]{3,2,1,0:T(8,128)(2,1)S(1)}, bf16[3,1,256,128]{3,2,1,0:T(8,128)(2,1)S(1)}, u32[]{:S(2)}, u32[]{:S(2)}) collective-permute-start(bf16[3,1,256,128]{3,2,1,0:T(8,128)(2,1)S(1)} %constant_dynamic-update-slice_fusion.9), channel_id=1, source_target_pairs={{1,0},{2,1},{3,2},{4,3},{5,4},{6,5},{7,6},{0,7},{9,8},{10,9},{11,1... | collective-permute-start | bytes 589832 | tf_op jit(solution)/shard_map/ppermute | solution.py:20
  47.3 2.0 copy-start.5
  49.3 3.6 %copy-start.3 = (f32[1,1,9,128,128]{4,3,2,1,0:T(8,128)S(1)}, f32[1,1,9,128,128]{4,3,2,1,0:T(8,128)}, u32[]{:S(2)}) copy-start(f32[1,1,9,128,128]{4,3,2,1,0:T(8,128)} %convert_element_type.43) | copy-start | bytes 1769476
  53.9 2.4 %copy-start.9 = (f32[32,128]{1,0:T(8,128)S(1)}, f32[32,128]{1,0:T(8,128)}, u32[]{:S(2)}) copy-start(f32[32,128]{1,0:T(8,128)} %copy-done.8) | copy-start | bytes 49156
  63.6 2.4 %copy-start.1 = (f32[32,128,128]{2,1,0:T(8,128)}, f32[32,128,128]{2,1,0:T(8,128)S(1)}, u32[]{:S(2)}) copy-start(f32[32,128,128]{2,1,0:T(8,128)S(1)} %multiply_reduce_fusion) | copy-start | bytes 6291460
  66.1 25.0 %copy-start.12 = (f32[16]{0:T(128)S(1)}, f32[16]{0:T(128)}, u32[]{:S(2)}) copy-start(f32[16]{0:T(128)} %copy-done.11) | copy-start | bytes 196
  89.0 2.1 copy-start.2
  89.1 10.7 %collective-permute-start.4 = (f32[1,3,256,128]{3,2,1,0:T(8,128)S(1)}, f32[1,3,256,128]{3,2,1,0:T(8,128)S(1)}, u32[]{:S(2)}, u32[]{:S(2)}) collective-permute-start(f32[1,3,256,128]{3,2,1,0:T(8,128)S(1)} %bitcast.174), channel_id=1, source_target_pairs={{0,8},{8,16},{16,24},{24,0},{1,9},{9,17},{17,25},{25,1},{2,10},{10... | collective-permute-start | bytes 1179656 | tf_op jit(solution)/shard_map/ppermute | solution.py:18
  89.2 10.6 %collective-permute-start.5 = (f32[1,3,256,128]{3,2,1,0:T(8,128)S(1)}, f32[1,3,256,128]{3,2,1,0:T(8,128)S(1)}, u32[]{:S(2)}, u32[]{:S(2)}) collective-permute-start(f32[1,3,256,128]{3,2,1,0:T(8,128)S(1)} %bitcast.173), channel_id=1, source_target_pairs={{8,0},{16,8},{24,16},{0,24},{9,1},{17,9},{25,17},{1,25},{10,2},{18... | collective-permute-start | bytes 1179656 | tf_op jit(solution)/shard_map/ppermute | solution.py:20
  92.5 10.6 %copy-start.10 = (f32[1,16,128]{2,1,0:T(8,128)S(1)}, f32[1,16,128]{2,1,0:T(8,128)}, u32[]{:S(2)}) copy-start(f32[1,16,128]{2,1,0:T(8,128)} %fusion.11) | copy-start | bytes 24580
  99.9 46.2 %collective-permute-start.6 = (f32[1,256,128]{2,1,0:T(8,128)S(1)}, f32[1,256,128]{2,1,0:T(8,128)S(1)}, u32[]{:S(2)}, u32[]{:S(2)}) collective-permute-start(f32[1,256,128]{2,1,0:T(8,128)S(1)} %get-tuple-element.16), channel_id=1, source_target_pairs={{0,1},{1,2},{2,3},{3,4},{4,5},{5,6},{6,7},{7,0},{8,9},{9,10},{10,1... | collective-permute-start | bytes 393224 | tf_op jit(solution)/shard_map/ppermute | solution.py:18
  102.4 43.7 %collective-permute-start.7 = (f32[1,256,128]{2,1,0:T(8,128)S(1)}, f32[1,256,128]{2,1,0:T(8,128)S(1)}, u32[]{:S(2)}, u32[]{:S(2)}) collective-permute-start(f32[1,256,128]{2,1,0:T(8,128)S(1)} %get-tuple-element.17), channel_id=1, source_target_pairs={{1,0},{2,1},{3,2},{4,3},{5,4},{6,5},{7,6},{0,7},{9,8},{10,9},{11,1... | collective-permute-start | bytes 393224 | tf_op jit(solution)/shard_map/ppermute | solution.py:20
Sparse Core Ops, SparseCore 0:
  103.2 125.4 all-reduce.1
where the time goes:
time: 238 us; the launch traced here: 237 us
  waiting for transfers between devices  98.2 us (41%)
  other arithmetic  45.1 us (19%)
  blocking collectives  43 us (18%)
  between operations  14.5 us (6%)
  matrix products  14.3 us (6%)
  local copies, waits for them, and re-layouts  14 us (6%)
  starting transfers between devices  8.19 us (3%)
    psum x1, waiting for transfers between devices, shards(): mix_total = lax.psum(mix_part, ('gz', 'xy'))  81.9 us
    psum x1, blocking collectives, shards(): radial_total = lax.psum(radial_part, ('gz', 'xy'))  43 us
    scatter-add x1, other arithmetic, shards(): grads = jnp.zeros((9 * natom, channels), jnp.float32).at[neighbour_local_...  22.9 us
    ppermute x4, waiting for transfers between devices, padded(): lax.ppermute(tail, axis, [(i, (i + 1) % count) for i in range(count)])  16.2 us
    dot_general x4, matrix products, exact(): return jnp.einsum(form, left, right, precision=lax.Precision.HIGHEST)  12.7 us
    gather x1, local copies, waits for them, and re-layouts, shards(): features = atom_table[neighbour_local_index].astype(jnp.float32)  12.1 us
    reduce_sum x2, other arithmetic, shards(): jnp.sum(angular[span_start:span_end, :, :, None] * dmoment_float[span_sta...  5.34 us
    reduce_sum x2, other arithmetic, shards(): jnp.sum(angular[span_start:span_end, :, :, None] * weighted[None], axis=1)  5.1 us
  transfers between devices with their start and end apart: 9, of which 3 were waited for; matrix products, arithmetic and copies ran while one was open for 6% of the time, Pallas kernels for 0%

commit v1 on v0

--- a/solution.py
+++ b/solution.py
@@ -117,7 +117,7 @@
         pieces.append(jnp.sum(angular[span_start:span_end, :, :, None] * weighted[None], axis=1))
     moments = jnp.concatenate(pieces, 0).astype(jnp.bfloat16)
     dmoments, mix_part = gate_backward(moments, mix_weight, cot_local)
-    mix_total = lax.psum(mix_part, ("gz", "xy"))
+    mix_total = lax.psum(lax.psum(mix_part, "xy"), "gz")
     dmoment_float = dmoments.astype(jnp.float32)
     contrib = jnp.zeros(features.shape, jnp.float32)
     radial_parts = []

time: 238 us -> 187 us (0.79)
  waiting for transfers between devices: 98.2 us -> 44.6 us
  other arithmetic: 45.1 us -> 47.9 us
    psum x1 -> x2, waiting for transfers between devices: 81.9 us -> 29.7 us  [shards(): mix_total = lax.psum(lax.psum(mix_part, 'xy'), 'gz')]
  transfers between devices with their start and end apart: 9 -> 10, of which waited for: 3 -> 3; matrix products, arithmetic and copies ran while one was open for 6% -> 26% of each run, Pallas kernels for 0% -> 0%
where the time goes in v1:
time: 187 us; the launch traced here: 185 us
  other arithmetic  47.9 us (26%)
  waiting for transfers between devices  44.6 us (24%)
  blocking collectives  43 us (23%)
  between operations  14.5 us (8%)
  local copies, waits for them, and re-layouts  14.2 us (8%)
  matrix products  13 us (7%)
  starting transfers between devices  8.21 us (4%)
    psum x1, blocking collectives, shards(): radial_total = lax.psum(radial_part, ('gz', 'xy'))  43 us
    psum x2, waiting for transfers between devices, shards(): mix_total = lax.psum(lax.psum(mix_part, 'xy'), 'gz')  29.7 us
    scatter-add x1, other arithmetic, shards(): grads = jnp.zeros((9 * natom, channels), jnp.float32).at[neighbour_local_...  22.9 us
    ppermute x4, waiting for transfers between devices, padded(): lax.ppermute(tail, axis, [(i, (i + 1) % count) for i in range(count)])  14.8 us
    gather x1, local copies, waits for them, and re-layouts, shards(): features = atom_table[neighbour_local_index].astype(jnp.float32)  12.1 us
    dot_general x4, matrix products, exact(): return jnp.einsum(form, left, right, precision=lax.Precision.HIGHEST)  11.3 us
    reduce_sum x2, other arithmetic, shards(): jnp.sum(angular[span_start:span_end, :, :, None] * dmoment_float[span_sta...  5.33 us
    reduce_sum x2, other arithmetic, shards(): jnp.sum(angular[span_start:span_end, :, :, None] * weighted[None], axis=1)  5.1 us
  transfers between devices with their start and end apart: 10, of which 3 were waited for; matrix products, arithmetic and copies ran while one was open for 26% of the time, Pallas kernels for 0%

profile of v1, /device:TPU:10, one launch (start us, length us, event | category | flops | bytes accessed | tf_op | source)
XLA Modules:
  0.0 185.4 jit_solution(9806665214811575056)
XLA Ops:
  7.2 0.0 copy-start
  7.2 0.0 all-reduce.3.cloned.1.call-start
  7.2 0.1 collective-permute-start
  7.3 1.7 collective-permute-start.1
  9.0 0.8 multiply_reduce_fusion.5
  9.9 0.7 fusion.78
  10.6 0.1 fusion.86
  10.7 1.3 compare_select_fusion
  12.1 0.0 copy-start.8
  12.1 0.0 copy-start.10
  12.1 0.0 copy-start.11
  12.1 7.2 %convolution_bitcast_fusion = f32[3,32,128,128]{3,2,0,1:T(8,128)} fusion(f32[32,128]{1,0:T(8,128)S(1)} %get-tuple-element.23, f32[16]{0:T(128)S(1)} %convert_multiply_fusion, f32[32,128]{1,0:T(8,128)S(1)} %get-tuple-element.22, f32[3,16,128]{2,1,0:T(8,128)S(1)} %copy-done), kind=kOutput, calls=%fused_computation.6 | convolution fusion | flops 302252032 | bytes 6348864 | tf_op jit(solution)/shard_map/bkp,lbc->lkpc/dot_general | solution.py:56
  19.4 0.9 convert_element_type.43
  20.2 0.0 collective-permute-done
  20.3 0.0 collective-permute-done.1
  20.3 1.6 collective-permute-start.2
  21.9 0.5 collective-permute-start.3
  22.4 8.9 %collective-permute-done.2 = bf16[3,1,256,128]{3,2,1,0:T(8,128)(2,1)S(1)} collective-permute-done((bf16[3,1,256,128]{3,2,1,0:T(8,128)(2,1)S(1)}, bf16[3,1,256,128]{3,2,1,0:T(8,128)(2,1)S(1)}, u32[]{:S(2)}, u32[]{:S(2)}) %collective-permute-start.2) | collective-permute-done | bytes 196640 | tf_op jit(solution)/shard_map/ppermute | solution.py:18
  31.3 0.0 collective-permute-done.3
  31.3 0.1 pad_maximum_fusion
  31.4 12.1 %gather_fusion = bf16[4096,128]{1,0:T(8,128)(2,1)S(1)} fusion(bf16[2304,128]{1,0:T(8,128)(2,1)S(1)} %bitcast.167, s32[4096]{0:T(1024)S(1)} %fusion.74), kind=kCustom, calls=%fused_computation | custom fusion | bytes 2113536 | tf_op jit(solution)/shard_map/gather | solution.py:112
  43.5 0.1 convert_element_type.49
  43.6 5.1 %fusion.83 = (f32[1,32,128,128]{3,2,0,1:T(8,128)}, bf16[128,128]{1,0:T(8,128)(2,1)S(1)}, f32[32,128,128]{2,1,0:T(8,128)S(1)}, f32[32,128,128]{2,1,0:T(8,128)S(1)...) fusion(f32[3,32,128,128]{3,2,0,1:T(8,128)} %convolution_bitcast_fusion, ...), kind=kLoop, calls=%fused_computation.141 | loop fusion | flops 3129344 | bytes 19972096 | tf_op jit(solution)/shard_map/slice | solution.py:129
  48.7 2.0 %multiply_reduce_fusion.3 = bf16[3,128,128]{2,1,0:T(8,128)(2,1)S(1)} fusion(f32[32,128,128]{2,1,0:T(8,128)S(1)} %get-tuple-element.8, f32[3,32,128]{2,1,0:T(8,128)S(1)} %slice.160), kind=kLoop, calls=%fused_computation.5 | loop fusion | flops 3096576 | bytes 2244608 | tf_op jit(solution)/shard_map/reduce_sum | solution.py:117
  50.8 0.2 fusion.54
  50.9 3.1 %multiply_reduce_fusion.1 = bf16[5,128,128]{2,1,0:T(8,128)(2,1)S(1)} fusion(f32[32,128,128]{2,1,0:T(8,128)S(1)} %get-tuple-element.7, f32[5,32,128]{2,1,0:T(8,128)S(1)} %slice.162), kind=kLoop, calls=%fused_computation.3 | loop fusion | flops 5160960 | bytes 2342912 | tf_op jit(solution)/shard_map/reduce_sum | solution.py:117
  54.0 0.2 fusion.48
  54.2 0.2 add_divide_fusion
  54.4 0.0 copy-done.7
  54.4 0.1 fusion.24
  54.5 0.2 convolution_bitcast_fusion.2
  54.7 0.2 convolution_bitcast_fusion.1
  55.0 0.1 fusion.52
  55.0 0.2 convolution_bitcast_fusion.3
  55.2 0.1 fusion.10
  55.3 0.2 convolution_convert_fusion
  55.6 0.2 convolution_convert_fusion.1
  55.8 0.7 pad_maximum_fusion.1
  56.5 0.0 all-reduce.3.cloned.1.call-update
  56.5 0.0 all-reduce.5.cloned.1.call-start
  56.6 2.1 %multiply_reduce_fusion.2 = f32[32,128,128]{2,1,0:T(8,128)S(1)} fusion(f32[3,128,128]{2,1,0:T(8,128)S(1)} %maximum_convert_fusion, f32[3,32,128]{2,1,0:T(8,128)S(1)} %slice.160), kind=kLoop, calls=%fused_computation.4 | loop fusion | flops 2621440 | bytes 2342912 | tf_op jit(solution)/shard_map/reduce_sum | solution.py:125
  58.7 3.2 %multiply_reduce_fusion = f32[32,128,128]{2,1,0:T(8,128)S(1)} fusion(f32[5,128,128]{2,1,0:T(8,128)S(1)} %fusion.27, f32[5,32,128]{2,1,0:T(8,128)S(1)} %slice.162), kind=kLoop, calls=%fused_computation.2 | loop fusion | flops 4718592 | bytes 2506752 | tf_op jit(solution)/shard_map/reduce_sum | solution.py:125
  62.0 3.7 %fusion = f32[4096,128]{1,0:T(8,128)} fusion(f32[32,128,128]{2,1,0:T(8,128)S(1)} %multiply_reduce_fusion, f32[1,32,128,128]{3,2,0,1:T(8,128)S(1)} %copy-done.6, f32[32,128,128]{2,1,0:T(8,128)S(1)} %multiply_reduce_fusion.2, f32[1,32,128,128]{3,2,0,1:T(8,128)} %get-tuple-element.10, f32[1,32,128,128]{3,2,0,1:T(8,128)S(1)} %copy-done.5, ...), kind=kLoop, calls=%fused_computation.8 | loop fusion | flops 3145728 | bytes 12664832 | tf_op jit(solution)/shard_map/add | solution.py:129
  65.7 0.0 copy-done.3
  65.7 22.9 %scatter_custom_fusion = f32[2304,128]{1,0:T(8,128)S(1)} fusion(s32[4096]{0:T(1024)} %bitcast.176, f32[4096,128]{1,0:T(8,128)} %fusion, f32[]{:T(128)} %constant.14.clone.1), kind=kCustom, calls=%fused_computation.36 | custom fusion | flops 524288 | bytes 1180160 | tf_op jit(solution)/shard_map/scatter-add | solution.py:134
  88.7 0.1 fusion.84
  88.8 0.1 collective-permute-start.4
  88.8 1.7 collective-permute-start.5
  90.6 1.3 fusion.14
  91.9 0.2 copy-done.4
  92.2 1.3 fusion.17
  93.5 6.0 %collective-permute-done.4 = f32[1,3,256,128]{3,2,1,0:T(8,128)S(1)} collective-permute-done((f32[1,3,256,128]{3,2,1,0:T(8,128)S(1)}, f32[1,3,256,128]{3,2,1,0:T(8,128)S(1)}, u32[]{:S(2)}, u32[]{:S(2)}) %collective-permute-start.4) | collective-permute-done | bytes 393248 | tf_op jit(solution)/shard_map/ppermute | solution.py:18
  99.5 0.0 collective-permute-done.5
  99.5 0.1 bitcast_add_fusion
  99.6 2.5 %collective-permute-start.6 = (f32[1,256,128]{2,1,0:T(8,128)S(1)}, f32[1,256,128]{2,1,0:T(8,128)S(1)}, u32[]{:S(2)}, u32[]{:S(2)}) collective-permute-start(f32[1,256,128]{2,1,0:T(8,128)S(1)} %get-tuple-element.16), channel_id=1, source_target_pairs={{0,1},{1,2},{2,3},{3,4},{4,5},{5,6},{6,7},{7,0},{8,9},{9,10},{10,1... | collective-permute-start | bytes 393224 | tf_op jit(solution)/shard_map/ppermute | solution.py:18
  102.0 0.0 collective-permute-start.7
  102.0 1.4 fusion.11
  103.5 43.0 %psum.21 = f32[3,16,128]{2,1,0:T(8,128)} all-reduce(f32[3,16,128]{2,1,0:T(8,128)S(1)} %pad_maximum_fusion.4), channel_id=1, replica_groups=mesh['gz'=4,'xy'=8] {'gz','xy'}, use_global_device_ids=true, to_apply=%region_8.0 | all-reduce | flops 6144 | bytes 49152 | tf_op jit(solution)/shard_map/psum | solution.py:137
  146.5 0.0 all-reduce.5.cloned.1.call-update
  146.5 0.0 collective-permute-done.6
  146.6 0.0 collective-permute-done.7
  146.6 0.7 fusion.29
  147.2 29.7 %all-reduce.5.cloned.1.call-done = f32[3,128,128]{2,1,0:T(8,128)} async-done(((f32[3,128,128]{2,1,0:T(8,128)}), f32[3,128,128]{2,1,0:T(8,128)}) %all-reduce.5.cloned.1.call-update) | async-done | bytes 196624 | tf_op jit(solution)/shard_map/psum | solution.py:120
  176.9 1.6 copy.29
  (41 shorter events, 0.2 us)
Async XLA Ops:
  7.2 4.9 %copy-start = (f32[3,16,128]{2,1,0:T(8,128)S(1)}, f32[3,16,128]{2,1,0:T(8,128)}, u32[]{:S(2)}) copy-start(f32[3,16,128]{2,1,0:T(8,128)} %param.12) | copy-start | bytes 73732
  7.2 139.3 %all-reduce.3.cloned.1.call-start = ((), (), s32[]{:S(2)}) async-start(), calls=%async_computation | async-start | bytes 393216 | tf_op jit(solution)/shard_map/psum | solution.py:120
  7.2 13.0 %collective-permute-start = (bf16[1,1,256,128]{3,2,1,0:T(8,128)(2,1)}, bf16[1,1,256,128]{3,2,1,0:T(8,128)(2,1)S(1)}, u32[]{:S(2)}, u32[]{:S(2)}) collective-permute-start(bf16[1,1,256,128]{3,2,1,0:T(8,128)(2,1)} %param.11), channel_id=1, source_target_pairs={{0,8},{8,16},{16,24},{24,0},{1,9},{9,17},{17,25},{25,1},{2,10},{10... | collective-permute-start | bytes 196616 | tf_op jit(solution)/shard_map/ppermute | solution.py:18
  7.3 13.0 %collective-permute-start.1 = (bf16[1,1,256,128]{3,2,1,0:T(8,128)(2,1)}, bf16[1,1,256,128]{3,2,1,0:T(8,128)(2,1)S(1)}, u32[]{:S(2)}, u32[]{:S(2)}) collective-permute-start(bf16[1,1,256,128]{3,2,1,0:T(8,128)(2,1)} %param.11), channel_id=1, source_target_pairs={{8,0},{16,8},{24,16},{0,24},{9,1},{17,9},{25,17},{1,25},{10,2},{18... | collective-permute-start | bytes 196616 | tf_op jit(solution)/shard_map/ppermute | solution.py:20
  12.1 7.3 %copy-start.8 = (bf16[1,1,9,128,128]{4,3,2,1,0:T(8,128)(2,1)S(1)}, bf16[1,1,9,128,128]{4,3,2,1,0:T(8,128)(2,1)}, u32[]{:S(2)}) copy-start(bf16[1,1,9,128,128]{4,3,2,1,0:T(8,128)(2,1)} %param.7) | copy-start | bytes 884740
  12.1 8.2 %copy-start.10 = (bf16[1,1,256,128]{3,2,1,0:T(8,128)(2,1)S(1)}, bf16[1,1,256,128]{3,2,1,0:T(8,128)(2,1)}, u32[]{:S(2)}) copy-start(bf16[1,1,256,128]{3,2,1,0:T(8,128)(2,1)} %param.11) | copy-start | bytes 196612
  12.1 10.3 %copy-start.11 = (s32[1,1,32,128]{3,2,1,0:T(8,128)S(1)}, s32[1,1,32,128]{3,2,1,0:T(8,128)}, u32[]{:S(2)}) copy-start(s32[1,1,32,128]{3,2,1,0:T(8,128)} %param.9) | copy-start | bytes 49156
  20.3 11.0 %collective-permute-start.2 = (bf16[3,1,256,128]{3,2,1,0:T(8,128)(2,1)S(1)}, bf16[3,1,256,128]{3,2,1,0:T(8,128)(2,1)S(1)}, u32[]{:S(2)}, u32[]{:S(2)}) collective-permute-start(bf16[3,1,256,128]{3,2,1,0:T(8,128)(2,1)S(1)} %constant_dynamic-update-slice_fusion.9), channel_id=1, source_target_pairs={{0,1},{1,2},{2,3},{3,4},{4,5},{5,6},{6,7},{7,0},{8,9},{9,10},{10,1... | collective-permute-start | bytes 589832 | tf_op jit(solution)/shard_map/ppermute | solution.py:18
  21.9 9.4 %collective-permute-start.3 = (bf16[3,1,256,128]{3,2,1,0:T(8,128)(2,1)S(1)}, bf16[3,1,256,128]{3,2,1,0:T(8,128)(2,1)S(1)}, u32[]{:S(2)}, u32[]{:S(2)}) collective-permute-start(bf16[3,1,256,128]{3,2,1,0:T(8,128)(2,1)S(1)} %constant_dynamic-update-slice_fusion.9), channel_id=1, source_target_pairs={{1,0},{2,1},{3,2},{4,3},{5,4},{6,5},{7,6},{0,7},{9,8},{10,9},{11,1... | collective-permute-start | bytes 589832 | tf_op jit(solution)/shard_map/ppermute | solution.py:20
  48.7 2.0 %copy-start.9 = (bf16[3,128,128]{2,1,0:T(8,128)(2,1)S(1)}, bf16[3,128,128]{2,1,0:T(8,128)(2,1)}, u32[]{:S(2)}) copy-start(bf16[3,128,128]{2,1,0:T(8,128)(2,1)} %param.13) | copy-start | bytes 294916
  50.8 3.6 %copy-start.7 = (f32[1,1,9,128,128]{4,3,2,1,0:T(8,128)S(1)}, f32[1,1,9,128,128]{4,3,2,1,0:T(8,128)}, u32[]{:S(2)}) copy-start(f32[1,1,9,128,128]{4,3,2,1,0:T(8,128)} %convert_element_type.43) | copy-start | bytes 1769476
  56.5 120.4 %all-reduce.5.cloned.1.call-start = ((), (), s32[]{:S(2)}) async-start(), calls=%async_computation.1 | async-start | bytes 393216 | tf_op jit(solution)/shard_map/psum | solution.py:120
  56.6 5.4 %copy-start.5 = (f32[1,32,128,128]{3,2,0,1:T(8,128)S(1)}, f32[1,32,128,128]{3,2,0,1:T(8,128)}, u32[]{:S(2)}) copy-start(f32[1,32,128,128]{3,2,0,1:T(8,128)} %get-tuple-element.5) | copy-start | bytes 6291460
  56.6 5.4 %copy-start.6 = (f32[1,32,128,128]{3,2,0,1:T(8,128)S(1)}, f32[1,32,128,128]{3,2,0,1:T(8,128)}, u32[]{:S(2)}) copy-start(f32[1,32,128,128]{3,2,0,1:T(8,128)} %get-tuple-element.9) | copy-start | bytes 6291460
  58.7 7.0 %copy-start.1 = (f32[32,128,128]{2,1,0:T(8,128)}, f32[32,128,128]{2,1,0:T(8,128)S(1)}, u32[]{:S(2)}) copy-start(f32[32,128,128]{2,1,0:T(8,128)S(1)} %multiply_reduce_fusion.2) | copy-start | bytes 6291460
  62.0 3.8 %copy-start.3 = (f32[32,128,128]{2,1,0:T(8,128)}, f32[32,128,128]{2,1,0:T(8,128)S(1)}, u32[]{:S(2)}) copy-start(f32[32,128,128]{2,1,0:T(8,128)S(1)} %multiply_reduce_fusion) | copy-start | bytes 6291460
  88.7 1.9 %copy-start.2 = (f32[32,128,128]{2,1,0:T(8,128)S(1)}, f32[32,128,128]{2,1,0:T(8,128)}, u32[]{:S(2)}) copy-start(f32[32,128,128]{2,1,0:T(8,128)} %copy-done.1) | copy-start | bytes 6291460
  88.8 10.7 %collective-permute-start.4 = (f32[1,3,256,128]{3,2,1,0:T(8,128)S(1)}, f32[1,3,256,128]{3,2,1,0:T(8,128)S(1)}, u32[]{:S(2)}, u32[]{:S(2)}) collective-permute-start(f32[1,3,256,128]{3,2,1,0:T(8,128)S(1)} %bitcast.174), channel_id=1, source_target_pairs={{0,8},{8,16},{16,24},{24,0},{1,9},{9,17},{17,25},{25,1},{2,10},{10... | collective-permute-start | bytes 1179656 | tf_op jit(solution)/shard_map/ppermute | solution.py:18
  88.8 10.6 %collective-permute-start.5 = (f32[1,3,256,128]{3,2,1,0:T(8,128)S(1)}, f32[1,3,256,128]{3,2,1,0:T(8,128)S(1)}, u32[]{:S(2)}, u32[]{:S(2)}) collective-permute-start(f32[1,3,256,128]{3,2,1,0:T(8,128)S(1)} %bitcast.173), channel_id=1, source_target_pairs={{8,0},{16,8},{24,16},{0,24},{9,1},{17,9},{25,17},{1,25},{10,2},{18... | collective-permute-start | bytes 1179656 | tf_op jit(solution)/shard_map/ppermute | solution.py:20
  90.6 1.6 copy-start.4
  99.6 47.0 %collective-permute-start.6 = (f32[1,256,128]{2,1,0:T(8,128)S(1)}, f32[1,256,128]{2,1,0:T(8,128)S(1)}, u32[]{:S(2)}, u32[]{:S(2)}) collective-permute-start(f32[1,256,128]{2,1,0:T(8,128)S(1)} %get-tuple-element.16), channel_id=1, source_target_pairs={{0,1},{1,2},{2,3},{3,4},{4,5},{5,6},{6,7},{7,0},{8,9},{9,10},{10,1... | collective-permute-start | bytes 393224 | tf_op jit(solution)/shard_map/ppermute | solution.py:18
  102.0 44.5 %collective-permute-start.7 = (f32[1,256,128]{2,1,0:T(8,128)S(1)}, f32[1,256,128]{2,1,0:T(8,128)S(1)}, u32[]{:S(2)}, u32[]{:S(2)}) collective-permute-start(f32[1,256,128]{2,1,0:T(8,128)S(1)} %get-tuple-element.17), channel_id=1, source_target_pairs={{1,0},{2,1},{3,2},{4,3},{5,4},{6,5},{7,6},{0,7},{9,8},{10,9},{11,1... | collective-permute-start | bytes 393224 | tf_op jit(solution)/shard_map/ppermute | solution.py:20
Sparse Core Ops, SparseCore 0:
  56.7 69.5 all-reduce.2
  146.7 30.1 all-reduce.4
